TPU v7x, 32 devices: a whole 2x2x4 slice. The times are simulated.
32 devices in a mesh: item: 8 (over z, x), store: 4 (over y, core).
Axes of the slice: x: 2, y: 2, z: 4, core: 2. Of those that a mesh axis runs over, the one named last changes fastest.
Arguments:
- predicted_units: bfloat16 [1024, 8, 2048], P('item', None, 'store'), may hold values from 0.049804688 to 5
- product_group: int32 [1024], P('item'), may hold values from 0 to 63, as said below
- product_goal: float32 [1024], P('item'), may hold values from 4915 to 49152
- group_outlet_goal: float32 [64, 2048], P(None, 'store'), may hold values from 38 to 384
- outlet_date_goal: float32 [8, 2048], P(None, 'store'), may hold values from 307 to 3072
Outputs:
- product_factor: float32 [1024], P('item')
- group_outlet_factor: float32 [64, 2048], P(None, 'store')
- outlet_date_factor: float32 [8, 2048], P(None, 'store')
- adjusted_tensor: bfloat16 [1024, 8, 2048], P('item', None, 'store')
Inputs may be any that keep to these rules, and one draw needn't show every extreme that they name: `product_group`: category ids never fall along the items, and every category holds at least 8 items; some category holds exactly that many.
All inputs are finite; a program needn't handle non-finite values.
Results may differ from a plain program's by a relative error of at most 0.001.
Values sent between devices are 32-bit elements; how exact they have to be, the bound alone decides.
A program may use at most 64 MiB of HBM per device.

v0:
```python
import jax
import jax.numpy as jnp
from jax import lax
from jax.sharding import PartitionSpec as P

ROUNDS = 4
INNER = 3


def shards(predicted_units, product_group, product_goal, group_outlet_goal, outlet_date_goal):
    product_slice, horizon_length, outlet_tally = predicted_units.shape
    cat_count = group_outlet_goal.shape[0]
    indicator_matrix = (
        product_group[:, None] == jnp.arange(cat_count, dtype=jnp.int32)[None, :]
    ).astype(jnp.float32)
    group_outlet_factor = jnp.ones((cat_count, outlet_tally), jnp.float32)
    outlet_date_factor = jnp.ones((horizon_length, outlet_tally), jnp.float32)

    def spread_tensor(multiplier):
        return jnp.dot(indicator_matrix, multiplier, precision=lax.Precision.HIGHEST)

    kept_multiplier = group_outlet_factor
    product_factor = jnp.ones((product_slice,), jnp.float32)
    for round_index in range(ROUNDS):
        masked_prediction = spread_tensor(kept_multiplier)[:, None, :] * outlet_date_factor[None]
        product_marginals = jnp.sum(predicted_units * masked_prediction, axis=(1, 2))
        product_factor = product_goal / lax.psum(product_marginals, "store")
        pooled_masked_prediction = predicted_units * product_factor[:, None, None]
        merged_matrix = lax.psum(
            jnp.einsum(
                "bv,bjz->vjz",
                indicator_matrix,
                pooled_masked_prediction,
                precision=lax.Precision.HIGHEST,
            ),
            "item",
        )
        for pass_index in range(INNER):
            kept_multiplier = group_outlet_goal / jnp.sum(
                merged_matrix * outlet_date_factor[None], axis=1
            )
            outlet_date_factor = outlet_date_goal / jnp.sum(
                merged_matrix * kept_multiplier[:, None, :], axis=0
            )
    adjusted_tensor = (
        predicted_units
        * product_factor[:, None, None]
        * spread_tensor(kept_multiplier)[:, None, :]
        * outlet_date_factor[None]
    ).astype(jnp.bfloat16)
    group_outlet_factor = kept_multiplier
    return (product_factor, group_outlet_factor, outlet_date_factor, adjusted_tensor)


def solution(mesh):
    in_specs = (P("item", None, "store"), P("item"), P("item"), P(None, "store"), P(None, "store"))
    out_specs = (P("item"), P(None, "store"), P(None, "store"), P("item", None, "store"))
    return jax.shard_map(shards, mesh=mesh, in_specs=in_specs, out_specs=out_specs, check_vma=False)
```

profile of v0, /device:TPU:0, one launch (start us, length us, event | category | flops | bytes accessed | tf_op | source)
XLA Modules:
  0.0 384.5 jit_solution(13354593638310893694)
XLA Ops:
  7.2 1.0 fusion.12
  8.3 2.3 fusion
  10.5 8.4 %psum.56 = f32[128]{0:T(128)S(1)} all-reduce(f32[128]{0:T(128)S(1)} %fusion), channel_id=1, replica_groups=mesh['item'=8,'store'=4] {'store'}, use_global_device_ids=true, to_apply=%region_1.0 | all-reduce | flops 128 | bytes 1024 | tf_op jit(solution)/shard_map/psum | solution.py:27
  18.9 0.7 div.84
  19.5 0.2 convert_multiply_fusion.6
  19.8 3.1 fusion.10
  22.9 78.6 %all-reduce.5.cloned.1.call-done = f32[64,8,512]{2,0,1:T(8,128)} async-done(((f32[64,8,512]{2,0,1:T(8,128)}), f32[64,8,512]{2,0,1:T(8,128)}) %all-reduce.5.cloned.1.call-update) | async-done | bytes 1048592 | tf_op jit(solution)/shard_map/psum | solution.py:29
  101.5 1.4 reduce_sum.253
  103.0 0.1 multiply_reduce_fusion.22
  103.2 0.1 multiply_reduce_fusion.21
  103.4 0.2 multiply_reduce_fusion.20
  103.5 0.1 multiply_reduce_fusion.19
  103.7 0.3 fusion.17
  104.0 0.2 multiply_reduce_fusion.18
  104.2 1.0 fusion.1
  105.3 5.9 %psum.58 = f32[128]{0:T(128)S(1)} all-reduce(f32[128]{0:T(128)S(1)} %fusion.1), channel_id=1, replica_groups=mesh['item'=8,'store'=4] {'store'}, use_global_device_ids=true, to_apply=%region_10.0 | all-reduce | flops 128 | bytes 1024 | tf_op jit(solution)/shard_map/psum | solution.py:27
  111.1 0.2 convert_multiply_fusion.4
  111.3 3.1 fusion.8
  114.5 77.8 %all-reduce.7.cloned.1.call-done = f32[64,8,512]{2,0,1:T(8,128)} async-done(((f32[64,8,512]{2,0,1:T(8,128)}), f32[64,8,512]{2,0,1:T(8,128)}) %all-reduce.7.cloned.1.call-update) | async-done | bytes 1048592 | tf_op jit(solution)/shard_map/psum | solution.py:29
  192.2 1.4 multiply_reduce_fusion.17
  193.8 0.1 multiply_reduce_fusion.16
  193.9 0.1 multiply_reduce_fusion.15
  194.1 0.2 multiply_reduce_fusion.14
  194.3 0.1 multiply_reduce_fusion.13
  194.4 0.3 fusion.15
  194.8 0.2 multiply_reduce_fusion.12
  194.9 1.0 fusion.2
  196.0 6.0 %psum.60 = f32[128]{0:T(128)S(1)} all-reduce(f32[128]{0:T(128)S(1)} %fusion.2), channel_id=1, replica_groups=mesh['item'=8,'store'=4] {'store'}, use_global_device_ids=true, to_apply=%region_19.0 | all-reduce | flops 128 | bytes 1024 | tf_op jit(solution)/shard_map/psum | solution.py:27
  202.0 0.2 convert_multiply_fusion.2
  202.3 3.1 fusion.6
  205.4 77.7 %all-reduce.9.cloned.1.call-done = f32[64,8,512]{2,0,1:T(8,128)} async-done(((f32[64,8,512]{2,0,1:T(8,128)}), f32[64,8,512]{2,0,1:T(8,128)}) %all-reduce.9.cloned.1.call-update) | async-done | bytes 1048592 | tf_op jit(solution)/shard_map/psum | solution.py:29
  283.1 1.4 multiply_reduce_fusion.11
  284.7 0.1 multiply_reduce_fusion.10
  284.8 0.1 multiply_reduce_fusion.9
  285.0 0.2 multiply_reduce_fusion.8
  285.3 0.3 fusion.14
  285.6 0.2 multiply_reduce_fusion.6
  285.8 1.0 fusion.3
  286.9 5.9 %psum.62 = f32[128]{0:T(128)S(1)} all-reduce(f32[128]{0:T(128)S(1)} %fusion.3), channel_id=1, replica_groups=mesh['item'=8,'store'=4] {'store'}, use_global_device_ids=true, to_apply=%region_28.0 | all-reduce | flops 128 | bytes 1024 | tf_op jit(solution)/shard_map/psum | solution.py:27
  292.7 0.2 convert_multiply_fusion
  293.0 3.1 fusion.4
  296.0 77.8 %all-reduce.11.cloned.1.call-done = f32[64,8,512]{2,0,1:T(8,128)} async-done(((f32[64,8,512]{2,0,1:T(8,128)}), f32[64,8,512]{2,0,1:T(8,128)}) %all-reduce.11.cloned.1.call-update) | async-done | bytes 1048592 | tf_op jit(solution)/shard_map/psum | solution.py:29
  373.8 1.4 multiply_reduce_fusion.5
  375.4 0.1 multiply_reduce_fusion.4
  375.7 0.2 multiply_reduce_fusion.2
  376.0 0.3 fusion.16
  376.4 0.2 multiply_reduce_fusion
  376.6 1.4 multiply_convert_fusion
  (62 shorter events, 1.4 us)
Async XLA Ops:
  7.2 12.4 %copy-start = (bf16[128,8,512]{2,1,0:T(8,128)(2,1)S(1)}, bf16[128,8,512]{2,1,0:T(8,128)(2,1)}, u32[]{:S(2)}) copy-start(bf16[128,8,512]{2,1,0:T(8,128)(2,1)} %param.5) | copy-start | bytes 3145732
  7.2 94.3 %all-reduce.5.cloned.1.call-start = ((), (), s32[]{:S(2)}) async-start(), calls=%async_computation | async-start | bytes 2097152 | tf_op jit(solution)/shard_map/psum | solution.py:29
  8.2 11.5 %copy-start.9 = (s32[128]{0:T(128)S(1)}, s32[128]{0:T(128)}, u32[]{:S(2)}) copy-start(s32[128]{0:T(128)} %param.6) | copy-start | bytes 1540
  19.8 83.1 %copy-start.5 = (f32[64,512]{1,0:T(8,128)S(1)}, f32[64,512]{1,0:T(8,128)}, u32[]{:S(2)}) copy-start(f32[64,512]{1,0:T(8,128)} %param.8) | copy-start | bytes 393220
  22.8 80.3 %copy-start.6 = (f32[8,512]{1,0:T(8,128)S(1)}, f32[8,512]{1,0:T(8,128)}, u32[]{:S(2)}) copy-start(f32[8,512]{1,0:T(8,128)} %param.9) | copy-start | bytes 49156
  22.9 169.4 %all-reduce.7.cloned.1.call-start = ((), (), s32[]{:S(2)}) async-start(), calls=%async_computation.1 | async-start | bytes 2097152 | tf_op jit(solution)/shard_map/psum | solution.py:29
  101.5 1.5 copy-start.1
  103.5 7.6 %copy-start.11 = (f32[128]{0:T(128)S(1)}, f32[128]{0:T(128)}, u32[]{:S(2)}) copy-start(f32[128]{0:T(128)} %param.7) | copy-start | bytes 1540
  114.4 168.7 %all-reduce.9.cloned.1.call-start = ((), (), s32[]{:S(2)}) async-start(), calls=%async_computation.2 | async-start | bytes 2097152 | tf_op jit(solution)/shard_map/psum | solution.py:29
  192.2 1.5 copy-start.2
  205.3 168.5 %all-reduce.11.cloned.1.call-start = ((), (), s32[]{:S(2)}) async-start(), calls=%async_computation.3 | async-start | bytes 2097152 | tf_op jit(solution)/shard_map/psum | solution.py:29
  283.1 1.5 copy-start.3
  292.7 83.8 %copy-start.10 = (f32[128]{0:T(128)}, f32[128]{0:T(128)S(1)}, u32[]{:S(2)}) copy-start(f32[128]{0:T(128)S(1)} %div.105) | copy-start | bytes 1540
  373.8 1.5 copy-start.4
  376.0 1.9 copy-start.7
  376.5 1.4 copy-start.8
Sparse Core Ops, SparseCore 0:
  23.0 78.4 all-reduce.4
  114.5 77.6 all-reduce.6
  205.5 77.6 all-reduce.8
  296.2 77.6 all-reduce.10
where the time goes:
time: 385 us; the launch traced here: 384 us
  waiting for transfers between devices  312 us (81%)
  blocking collectives  26.1 us (7%)
  other arithmetic  17.2 us (4%)
  matrix products  14.5 us (4%)
  between operations  14.3 us (4%)
    psum x4, waiting for transfers between devices, shards(): lax.psum(jnp.einsum('bv,bjz->vjz', indicator_matrix, pooled_masked_predic...  312 us
    psum x4, blocking collectives, shards(): product_factor = product_goal / lax.psum(product_marginals, 'store')  26.1 us
    dot_general x4, matrix products, shards(): jnp.einsum('bv,bjz->vjz', indicator_matrix, pooled_masked_prediction, pre...  12.2 us
  transfers between devices with their start and end apart: 4, of which 4 were waited for; matrix products, arithmetic and copies ran while one was open for 0% of the time, Pallas kernels for 0%

commit v1 on v0

v1 whole, which is shorter than its diff:
```python
import functools

import jax
import jax.numpy as jnp
from jax import lax
from jax.experimental import pallas as pl
from jax.experimental.pallas import tpu as pltpu
from jax.sharding import PartitionSpec as P

ROUNDS = 4
INNER = 3
LANES = 128
MESH = pl.DeviceIdType.MESH


def up(value, multiple):
    return -(-value // multiple) * multiple


def split(value):
    high = value.astype(jnp.bfloat16).astype(jnp.float32)
    return high, value - high


def kernel(n_item, n_store, local, first_ref, x_ref, group_ref, goal_ref, cat_goal_ref, date_goal_ref,
           factor_ref, cat_ref, date_ref, out_ref,
           cat_all, pool, scatter_out, scatter_in, solved_out, solved_in, date_pack, place,
           row_out, row_in, meta_out, meta_in,
           scatter_ssem, scatter_rsem, solved_ssem, solved_rsem, row_ssem, row_rsem, meta_ssem, meta_rsem):
    days, items, stores = x_ref.shape
    cats = cat_goal_ref.shape[0]
    chunk = stores // n_item
    per_block = LANES // chunk
    blocks = stores // LANES
    rows_day = days // per_block
    rows_cat = cats // per_block
    sent_rows = scatter_out.shape[1]
    me = lax.axis_index("item")
    mine = lax.axis_index("store")
    f32, bf16 = jnp.float32, jnp.bfloat16

    barrier = pltpu.get_barrier_semaphore()
    for off in range(1, n_item):
        pl.semaphore_signal(barrier, inc=1, device_id={"item": lax.rem(me + off, n_item)}, device_id_type=MESH)
    for off in range(1, n_store):
        pl.semaphore_signal(barrier, inc=1, device_id={"store": lax.rem(mine + off, n_store)}, device_id_type=MESH)

    first = first_ref[0]
    lane_group = lambda rows: lax.broadcasted_iota(jnp.int32, (rows, LANES), 1) // chunk

    def roll(value, groups):
        shift = (groups * chunk) % LANES
        return value if shift == 0 else pltpu.roll(value, shift, 1)

    def pack(parts, at):
        total = roll(parts[0], -at)
        for g in range(1, per_block):
            total = jnp.where(lane_group(total.shape[0]) == g, roll(parts[g], g - at), total)
        return total

    def unpack(parts, at):
        total = roll(parts[0], -at)
        for h in range(1, per_block):
            total = jnp.where(lane_group(total.shape[0]) == h, roll(parts[h], h - at), total)
        return total

    def to_item(src, dst, ssem, rsem, off):
        peer = lax.rem(me + off, n_item)
        return pltpu.make_async_remote_copy(
            src_ref=src(peer), dst_ref=dst(me), send_sem=ssem.at[peer], recv_sem=rsem.at[me],
            device_id={"item": peer}, device_id_type=MESH)

    def from_item(src, dst, ssem, rsem, off):
        peer = lax.rem(me + off, n_item)
        return pltpu.make_async_remote_copy(
            src_ref=src(peer), dst_ref=dst(peer), send_sem=ssem.at[peer], recv_sem=rsem.at[peer],
            device_id={"item": peer}, device_id_type=MESH)

    meta = (lambda j: meta_out, lambda j: meta_in.at[j], meta_ssem, meta_rsem)
    scatter = (lambda j: scatter_out.at[j], lambda j: scatter_in.at[j, pl.ds(0, sent_rows)], scatter_ssem, scatter_rsem)
    solved = (lambda j: solved_out, lambda j: solved_in.at[j], solved_ssem, solved_rsem)

    local_id = group_ref[...] - first
    onehot = (local_id == lax.broadcasted_iota(jnp.int32, (local, items), 0)).astype(f32)
    meta_out[...] = jnp.full(meta_out.shape, first.astype(f32))
    meta_in[pl.ds(me, 1)] = meta_out[...][None]
    scatter_in[...] = jnp.zeros(scatter_in.shape, f32)
    scatter_out[...] = jnp.zeros(scatter_out.shape, f32)
    solved_out[...] = jnp.zeros(solved_out.shape, f32)
    cat_all[...] = jnp.ones(cat_all.shape, f32)
    date_ref[...] = jnp.ones(date_ref.shape, f32)
    date_pack[...] = jnp.ones(date_pack.shape, f32)
    block_at = pl.multiple_of((me // per_block) * LANES, LANES)
    group_at = lax.rem(me, per_block)
    cat_goal_all = cat_goal_ref[:, pl.ds(block_at, LANES)]
    date_goal_all = date_goal_ref[:, pl.ds(block_at, LANES)]
    cat_goal = jnp.zeros((cats, LANES), f32)
    date_goal = jnp.zeros((rows_day, LANES), f32)
    for h in range(per_block):
        here = group_at == h
        cat_goal = jnp.where(here, pack([cat_goal_all] * per_block, h), cat_goal)
        date_parts = [date_goal_all[g * rows_day:(g + 1) * rows_day] for g in range(per_block)]
        date_goal = jnp.where(here, pack(date_parts, h), date_goal)

    pl.semaphore_wait(barrier, n_item + n_store - 2)
    for off in range(1, n_item):
        to_item(*meta, off).start()
    for off in range(1, n_item):
        from_item(*meta, off).wait_recv()
    for off in range(1, n_item):
        to_item(*meta, off).wait_send()

    row_index = lax.broadcasted_iota(jnp.int32, (rows_day * cats, LANES), 0)
    lane_index = lax.broadcasted_iota(jnp.int32, (rows_day * cats, LANES), 1)
    sent_cats = min(cats, (items - 2) // max(1, items * n_item // (2 * cats)) + 2)
    offset = lane_index - (row_index // cats) * sent_cats
    inside = (offset >= 0) & (offset < sent_cats)
    wanted = (row_index % cats - offset).astype(f32)
    for j in range(n_item):
        hit = inside & (wanted == meta_in[j][0:1, :])
        place[:, j * LANES:(j + 1) * LANES] = jnp.where(hit, 1.0, 0.0).astype(bf16)

    def own_cats():
        return jnp.concatenate([cat_all[b, pl.ds(first, local), :] for b in range(blocks)], axis=1)

    def one_round(index, carry):
        chosen = own_cats()
        sums = jnp.zeros((2 * local, items), f32)
        for d in range(days):
            high, low = split(chosen * date_ref[d:d + 1, :])
            weight = jnp.concatenate([high, low], axis=0).astype(bf16)
            sums = sums + lax.dot_general(weight, x_ref[d], (((1,), (1,)), ((), ())), preferred_element_type=f32)
        row_sum = jnp.sum(onehot * (sums[:local] + sums[local:]), axis=0, keepdims=True)
        row_out[index] = jnp.broadcast_to(row_sum, (8, items))

        def row_copy(off, arriving):
            peer = lax.rem(mine + off, n_store)
            slot = peer if arriving else mine
            return pltpu.make_async_remote_copy(
                src_ref=row_out.at[index], dst_ref=row_in.at[index, slot],
                send_sem=row_ssem.at[index, peer], recv_sem=row_rsem.at[index, slot],
                device_id={"store": peer}, device_id_type=MESH)

        for off in range(1, n_store):
            row_copy(off, False).start()
        row_in[index, mine] = jnp.broadcast_to(row_sum, (8, items))
        for off in range(1, n_store):
            row_copy(off, True).wait_recv()
        whole = row_in[index, 0]
        for t in range(1, n_store):
            whole = whole + row_in[index, t]
        factor = goal_ref[...] / whole[0:1, :]
        factor_ref[...] = factor

        high, low = split(onehot * factor)
        weight = jnp.concatenate([high, low], axis=0).astype(bf16)
        for d in range(days):
            both = jnp.dot(weight, x_ref[d], preferred_element_type=f32)
            pool[d] = both[:local] + both[local:]
        for j in range(n_item):
            b, h = j // per_block, j % per_block
            for row in range(rows_day):
                parts = [pool[g * rows_day + row, :, b * LANES:(b + 1) * LANES] for g in range(per_block)]
                scatter_out[j, row * sent_cats:(row + 1) * sent_cats, :] = pack(parts, h)[:sent_cats]
        for off in range(1, n_item):
            to_item(*scatter, off).start()
        scatter_in[pl.ds(me, 1), 0:sent_rows, :] = scatter_out[pl.ds(me, 1)]
        for off in range(1, n_item):
            from_item(*scatter, off).wait_recv()

        arrived = scatter_in[...].reshape(n_item * LANES, LANES)
        high, low = split(arrived)
        both = jnp.dot(place[...], jnp.concatenate([high, low], axis=1).astype(bf16), preferred_element_type=f32)
        merged = both[:, :LANES] + both[:, LANES:]
        pooled = [merged[row * cats:(row + 1) * cats] for row in range(rows_day)]
        dates = [date_pack[row:row + 1, :] for row in range(rows_day)]
        cat = cat_goal
        for _ in range(INNER):
            below = pooled[0] * dates[0]
            for row in range(1, rows_day):
                below = below + pooled[row] * dates[row]
            total = below
            for g in range(1, per_block):
                total = total + roll(below, g)
            cat = cat_goal / total
            dates = [date_goal[row:row + 1] / jnp.sum(cat * pooled[row], axis=0, keepdims=True)
                     for row in range(rows_day)]
        for row in range(rows_day):
            date_pack[row:row + 1, :] = dates[row]
            solved_out[rows_cat + row:rows_cat + row + 1, :] = dates[row]
        packed = cat[:rows_cat]
        for g in range(1, per_block):
            packed = jnp.where(lane_group(rows_cat) == g, cat[g * rows_cat:(g + 1) * rows_cat], packed)
        solved_out[0:rows_cat, :] = packed
        for off in range(1, n_item):
            to_item(*solved, off).start()
        solved_in[pl.ds(me, 1)] = solved_out[...][None]
        for off in range(1, n_item):
            from_item(*solved, off).wait_recv()
        for b in range(blocks):
            sources = [solved_in[b * per_block + h] for h in range(per_block)]
            for g in range(per_block):
                whole_rows = unpack(sources, g)
                cat_all[b, g * rows_cat:(g + 1) * rows_cat, :] = whole_rows[:rows_cat]
                date_ref[g * rows_day:(g + 1) * rows_day, b * LANES:(b + 1) * LANES] = (
                    whole_rows[rows_cat:rows_cat + rows_day])
        for off in range(1, n_store):
            row_copy(off, False).wait_send()
        for off in range(1, n_item):
            to_item(*scatter, off).wait_send()
            to_item(*solved, off).wait_send()
        return carry

    lax.fori_loop(0, ROUNDS, one_round, 0)

    for b in range(blocks):
        cat_ref[:, b * LANES:(b + 1) * LANES] = cat_all[b, 0:cats, :]
    by_item = jnp.concatenate([onehot, jnp.zeros((items - local, items), f32)], axis=0).T
    factor_column = jnp.broadcast_to(factor_ref[...], (items, items)).T
    chosen = jnp.concatenate([own_cats(), jnp.zeros((items - local, stores), f32)], axis=0)
    spread = jnp.dot(by_item, chosen, precision=lax.Precision.HIGHEST, preferred_element_type=f32)
    scaled = spread * factor_column[:, 0:1]
    for d in range(days):
        out_ref[d] = (x_ref[d].astype(f32) * scaled * date_ref[d:d + 1, :]).astype(bf16)


def shards(n_item, n_store, predicted_units, product_group, product_goal, group_outlet_goal, outlet_date_goal):
    items, days, stores = predicted_units.shape
    cats = group_outlet_goal.shape[0]
    least = max(1, items * n_item // (2 * cats))
    sent_cats = min(cats, (items - 2) // least + 2)
    local = up(sent_cats, 8)
    per_block = LANES // (stores // n_item)
    rows_day = days // per_block
    sent_rows = up(rows_day * sent_cats, 8)
    solved_rows = up(cats // per_block + rows_day, 8)
    f32 = jnp.float32
    vmem = pl.BlockSpec(memory_space=pltpu.VMEM)
    dma = pltpu.SemaphoreType.DMA
    factor, cat, date, out = pl.pallas_call(
        functools.partial(kernel, n_item, n_store, local),
        out_shape=(
            jax.ShapeDtypeStruct((1, items), f32),
            jax.ShapeDtypeStruct((cats, stores), f32),
            jax.ShapeDtypeStruct((days, stores), f32),
            jax.ShapeDtypeStruct((days, items, stores), jnp.bfloat16),
        ),
        in_specs=[pl.BlockSpec(memory_space=pltpu.SMEM)] + [vmem] * 5,
        out_specs=(vmem,) * 4,
        scratch_shapes=[
            pltpu.VMEM((stores // LANES, cats + local, LANES), f32),
            pltpu.VMEM((days, local, stores), f32),
            pltpu.VMEM((n_item, sent_rows, LANES), f32),
            pltpu.VMEM((n_item, LANES, LANES), f32),
            pltpu.VMEM((solved_rows, LANES), f32),
            pltpu.VMEM((n_item, solved_rows, LANES), f32),
            pltpu.VMEM((up(rows_day, 8), LANES), f32),
            pltpu.VMEM((rows_day * cats, n_item * LANES), jnp.bfloat16),
            pltpu.VMEM((ROUNDS, 8, items), f32),
            pltpu.VMEM((ROUNDS, n_store, 8, items), f32),
            pltpu.VMEM((8, LANES), f32),
            pltpu.VMEM((n_item, 8, LANES), f32),
            dma((n_item,)), dma((n_item,)), dma((n_item,)), dma((n_item,)),
            dma((ROUNDS, n_store)), dma((ROUNDS, n_store)), dma((n_item,)), dma((n_item,)),
        ],
        compiler_params=pltpu.CompilerParams(
            collective_id=0, has_side_effects=True, vmem_limit_bytes=40 * 1024 * 1024),
    )(product_group[:1], predicted_units.transpose(1, 0, 2), product_group[None], product_goal[None],
      group_outlet_goal, outlet_date_goal)
    return factor[0], cat, date, out.transpose(1, 0, 2)


def solution(mesh):
    in_specs = (P("item", None, "store"), P("item"), P("item"), P(None, "store"), P(None, "store"))
    out_specs = (P("item"), P(None, "store"), P(None, "store"), P("item", None, "store"))
    body = functools.partial(shards, mesh.shape["item"], mesh.shape["store"])
    return jax.shard_map(body, mesh=mesh, in_specs=in_specs, out_specs=out_specs, check_vma=False)
```

time: 385 us -> 89.9 us (0.23)
  waiting for transfers between devices: 312 us -> 0 us
  Pallas kernels: 0 us -> 83.5 us
  blocking collectives: 26.1 us -> 0 us
  other arithmetic: 17.2 us -> 0 us
  matrix products: 14.5 us -> 0 us
  between operations: 14.3 us -> 0.69 us
  local copies, waits for them, and re-layouts: 0.33 us -> 5.54 us
    psum x4 -> x0, waiting for transfers between devices: 312 us -> none  [shards(): lax.psum(jnp.einsum('bv,bjz->vjz', indicator_matrix, pooled_masked_predic...]
    pallas_call x0 -> x1, Pallas kernels: none -> 83.5 us  [shards(): pl.pallas_call(functools.partial(kernel, n_item, n_store, local), out_sha...]
    psum x4 -> x0, blocking collectives: 26.1 us -> none  [shards(): product_factor = product_goal / lax.psum(product_marginals, 'store')]
    dot_general x9 -> x0, matrix products: 14.5 us -> none  [the longest x4 12.2 us: shards(): jnp.einsum('bv,bjz->vjz', indicator_matrix, pooled_masked_prediction, pre...]
    reduce_sum x28 -> x0, other arithmetic: 13.9 us -> none  [the longest x12 6.7 us: shards(): jnp.sum(merged_matrix * outlet_date_factor[None], axis=1)]
    unnamed x24 -> x13, local copies, waits for them, and re-layouts: 0.33 us -> 5.54 us
  transfers between devices with their start and end apart: 4 -> 0, of which waited for: 4 -> 0; matrix products, arithmetic and copies ran while one was open for 0% -> 0% of each run, Pallas kernels for 0% -> 0%
where the time goes in v1:
time: 89.9 us; the launch traced here: 89.7 us
  Pallas kernels  83.5 us (93%)
  local copies, waits for them, and re-layouts  5.54 us (6%)
    pallas_call x1, Pallas kernels, shards(): pl.pallas_call(functools.partial(kernel, n_item, n_store, local), out_sha...  83.5 us
    unnamed x13, local copies, waits for them, and re-layouts  5.54 us

profile of v1, /device:TPU:0, one launch (start us, length us, event | category | flops | bytes accessed | tf_op | source)
XLA Modules:
  0.0 89.7 jit_solution(13789145286327195083)
XLA Ops:
  0.6 0.0 copy-start
  0.6 0.0 copy-start.1
  0.7 1.6 %copy.12 = bf16[128,8,512]{2,0,1:T(8,128)(2,1)S(1)} copy(bf16[128,8,512]{2,1,0:T(8,128)(2,1)} %param.5) | data formatting | bytes 2097152 | tf_op args[0]
  2.2 0.0 copy-start.2
  2.2 0.0 copy-start.3
  2.2 0.0 copy-done
  2.3 0.0 copy-done.1
  2.3 0.6 copy-done.2
  2.9 0.0 copy-done.3
  2.9 83.5 %shard_map.84 = (f32[1,128]{1,0:T(1,128)S(1)}, f32[64,512]{1,0:T(8,128)S(1)}, f32[8,512]{1,0:T(8,128)S(1)}, bf16[8,128,512]{2,1,0:T(8,128)(2,1)S(1)}) custom-call(s32[1]{0:T(128)S(1)} %bitcast.10, bf16[8,128,512]{2,1,0:T(8,128)(2,1)S(1)} %bitcast.8, s32[1,128]{1,0:T(1,128)S(1)} %bitcast.11, f32[1,128]{1,0:T(1,128)S(1)} %bitcast.12, f32[64,512]{1,0:T(8,128)S(1)} %copy-done, ...), custom_call_target="tpu_custom_call" | custom-call | tf_op jit(solution)/shard_map/pallas_call | solution.py:240
  86.4 1.5 %copy.10 = bf16[128,8,512]{2,1,0:T(8,128)(2,1)} copy(bf16[128,8,512]{2,0,1:T(8,128)(2,1)S(1)} %bitcast.9) | data formatting | bytes 2097152
  87.9 0.5 copy.16
  88.4 0.7 copy.17
  89.1 0.6 copy.18
Async XLA Ops:
  0.6 1.6 %copy-start = (f32[64,512]{1,0:T(8,128)S(1)}, f32[64,512]{1,0:T(8,128)}, u32[]{:S(2)}) copy-start(f32[64,512]{1,0:T(8,128)} %cat_goal_ref.1) | copy-start | bytes 393220
  0.6 1.6 %copy-start.1 = (f32[8,512]{1,0:T(8,128)S(1)}, f32[8,512]{1,0:T(8,128)}, u32[]{:S(2)}) copy-start(f32[8,512]{1,0:T(8,128)} %date_goal_ref.1) | copy-start | bytes 49156
  2.2 0.7 copy-start.2
  2.2 0.7 copy-start.3

commit v2 on v1

v2 whole, which is shorter than its diff:
```python
import functools

import jax
import jax.numpy as jnp
from jax import lax
from jax.experimental import pallas as pl
from jax.experimental.pallas import tpu as pltpu
from jax.sharding import PartitionSpec as P

ROUNDS = 4
INNER = 3
LANES = 128
MESH = pl.DeviceIdType.MESH


def up(value, multiple):
    return -(-value // multiple) * multiple


def split(value):
    high = value.astype(jnp.bfloat16).astype(jnp.float32)
    return high, value - high


def kernel(n_item, n_store, sent_cats, x_ref, group_ref, first_ref, goal_ref, cat_goal_ref, date_goal_ref,
           factor_ref, cat_ref, date_ref, out_ref,
           chosen_all, date_all, cat_all, scatter_out, scatter_in, part_out, part_in, solved_out, solved_in,
           date_pack, place, select, row_out, row_in, meta_out, meta_in,
           scatter_ssem, scatter_rsem, part_ssem, part_rsem, solved_ssem, solved_rsem,
           row_ssem, row_rsem, meta_ssem, meta_rsem):
    days, items, stores = x_ref.shape
    cats = cat_goal_ref.shape[0]
    local = chosen_all.shape[1]
    chunk = stores // n_item
    per_block = LANES // chunk
    blocks = stores // LANES
    rows_day = days // per_block
    rows_cat = cats // per_block
    rows_part = up(sent_cats, per_block) // per_block
    rows_select = up(rows_part, 8)
    sent_rows = scatter_out.shape[1]
    me = lax.axis_index("item")
    mine = lax.axis_index("store")
    my_block = me // per_block
    near = sorted(range(blocks), key=lambda t: (min(t, blocks - t), t))
    f32, bf16 = jnp.float32, jnp.bfloat16

    barrier = pltpu.get_barrier_semaphore()
    for off in range(1, n_item):
        pl.semaphore_signal(barrier, inc=1, device_id={"item": lax.rem(me + off, n_item)}, device_id_type=MESH)
    for off in range(1, n_store):
        pl.semaphore_signal(barrier, inc=1, device_id={"store": lax.rem(mine + off, n_store)}, device_id_type=MESH)

    lane_group = lambda rows: lax.broadcasted_iota(jnp.int32, (rows, LANES), 1) // chunk

    def roll(value, groups):
        shift = (groups * chunk) % LANES
        return value if shift == 0 else pltpu.roll(value, shift, 1)

    def pack(parts, at):
        total = roll(parts[0], -at)
        for g in range(1, per_block):
            total = jnp.where(lane_group(total.shape[0]) == g, roll(parts[g], g - at), total)
        return total

    def unpack(parts, at):
        total = roll(parts[0], -at)
        for h in range(1, per_block):
            total = jnp.where(lane_group(total.shape[0]) == h, roll(parts[h], h - at), total)
        return total

    def item_copy(kind, peer, arriving):
        src, dst, ssem, rsem = kind
        slot = peer if arriving else me
        return pltpu.make_async_remote_copy(
            src_ref=src(peer), dst_ref=dst(slot), send_sem=ssem.at[peer], recv_sem=rsem.at[slot],
            device_id={"item": peer}, device_id_type=MESH)

    def send(kind, peer):
        pl.when(peer != me)(lambda: item_copy(kind, peer, False).start())

    def receive(kind, peer):
        pl.when(peer != me)(lambda: item_copy(kind, peer, True).wait_recv())

    def sent(kind):
        for off in range(1, n_item):
            item_copy(kind, lax.rem(me + off, n_item), False).wait_send()

    def block_of(t):
        return lax.rem(my_block + t, blocks)

    meta = (lambda j: meta_out, lambda j: meta_in.at[j], meta_ssem, meta_rsem)
    scatter = (lambda j: scatter_out.at[j], lambda j: scatter_in.at[j, pl.ds(0, sent_rows)], scatter_ssem, scatter_rsem)
    part = (lambda j: part_out.at[j], lambda j: part_in.at[j], part_ssem, part_rsem)
    solved = (lambda j: solved_out, lambda j: solved_in.at[j], solved_ssem, solved_rsem)

    def row_copy(index, off, arriving):
        peer = lax.rem(mine + off, n_store)
        slot = peer if arriving else mine
        return pltpu.make_async_remote_copy(
            src_ref=row_out.at[index], dst_ref=row_in.at[index, slot],
            send_sem=row_ssem.at[index, peer], recv_sem=row_rsem.at[index, slot],
            device_id={"store": peer}, device_id_type=MESH)

    first = first_ref[...]
    onehot = (group_ref[...] - first == lax.broadcasted_iota(jnp.int32, (local, items), 0)).astype(f32)

    def x_block(b, axis):
        at = pl.ds(pl.multiple_of(b * LANES, LANES), LANES)
        return jnp.concatenate([x_ref[d, :, at] for d in range(days)], axis=axis)

    def block_sums(b):
        chosen, date = chosen_all[b], date_all[b]
        high, low = split(jnp.concatenate([chosen * date[d:d + 1, :] for d in range(days)], axis=1))
        weight = jnp.concatenate([high, low], axis=0).astype(bf16)
        return lax.dot_general(weight, x_block(b, 1), (((1,), (1,)), ((), ())), preferred_element_type=f32)

    def send_rows(index, sums):
        row_sum = jnp.sum(onehot * (sums[:local] + sums[local:]), axis=0, keepdims=True)
        row_out[index] = jnp.broadcast_to(row_sum, (8, items))
        for off in range(1, n_store):
            row_copy(index, off, False).start()
        row_in[index, mine] = jnp.broadcast_to(row_sum, (8, items))

    meta_out[...] = jnp.broadcast_to(first.astype(f32), meta_out.shape)
    meta_in[pl.ds(me, 1)] = meta_out[...][None]
    scatter_in[...] = jnp.zeros(scatter_in.shape, f32)
    scatter_out[...] = jnp.zeros(scatter_out.shape, f32)
    part_out[...] = jnp.zeros(part_out.shape, f32)
    solved_out[...] = jnp.zeros(solved_out.shape, f32)
    chosen_all[...] = jnp.ones(chosen_all.shape, f32)
    date_all[...] = jnp.ones(date_all.shape, f32)
    date_pack[...] = jnp.ones(date_pack.shape, f32)
    sums = block_sums(0)
    for b in range(1, blocks):
        sums = sums + block_sums(b)
    pl.semaphore_wait(barrier, n_item + n_store - 2)
    for off in range(1, n_item):
        send(meta, lax.rem(me + off, n_item))
    send_rows(0, sums)

    block_at = pl.multiple_of(my_block * LANES, LANES)
    group_at = lax.rem(me, per_block)
    cat_goal_all = cat_goal_ref[:, pl.ds(block_at, LANES)]
    date_goal_all = date_goal_ref[:, pl.ds(block_at, LANES)]
    cat_goal = jnp.zeros((cats, LANES), f32)
    date_goal = jnp.zeros((rows_day, LANES), f32)
    for h in range(per_block):
        here = group_at == h
        cat_goal = jnp.where(here, pack([cat_goal_all] * per_block, h), cat_goal)
        date_parts = [date_goal_all[g * rows_day:(g + 1) * rows_day] for g in range(per_block)]
        date_goal = jnp.where(here, pack(date_parts, h), date_goal)

    for off in range(1, n_item):
        receive(meta, lax.rem(me + off, n_item))
    sent(meta)
    row_index = lax.broadcasted_iota(jnp.int32, (rows_day * cats, LANES), 0)
    lane_index = lax.broadcasted_iota(jnp.int32, (rows_day * cats, LANES), 1)
    offset = lane_index - (row_index // cats) * sent_cats
    inside = (offset >= 0) & (offset < sent_cats)
    wanted = (row_index % cats - offset).astype(f32)
    part_index = lax.broadcasted_iota(jnp.int32, (per_block * rows_select, cats), 0)
    cat_index = lax.broadcasted_iota(jnp.int32, (per_block * rows_select, cats), 1)
    part_row = part_index % rows_select
    part_wanted = (cat_index - (part_index // rows_select) * rows_part - part_row).astype(f32)
    for j in range(n_item):
        start = meta_in[j][0:1, :]
        hit = inside & (wanted == start)
        at = (j % per_block) * LANES
        place[j // per_block, :, at:at + LANES] = jnp.where(hit, 1.0, 0.0).astype(bf16)
        hit = (part_row < rows_part) & (part_wanted == start[:, :cats])
        height = per_block * rows_select
        select[j * height:(j + 1) * height, :] = jnp.where(hit, 1.0, 0.0).astype(bf16)

    def fit(index):
        for off in range(1, n_store):
            row_copy(index, off, True).wait_recv()
        whole = row_in[index, 0]
        for t in range(1, n_store):
            whole = whole + row_in[index, t]
        factor = goal_ref[...] / whole[0:1, :]
        factor_ref[...] = factor

        high, low = split(onehot * factor)
        weight = jnp.concatenate([high, low], axis=0).astype(bf16)
        for t in reversed(near):
            b = block_of(t)
            both = jnp.dot(weight, x_block(b, 1), preferred_element_type=f32)
            pool = both[:local] + both[local:]
            for h in range(per_block):
                j = b * per_block + h
                for row in range(rows_day):
                    at = [(g * rows_day + row) * LANES for g in range(per_block)]
                    packed = pack([pool[:, i:i + LANES] for i in at], h)
                    scatter_out[j, row * sent_cats:(row + 1) * sent_cats, :] = packed[:sent_cats]
                send(scatter, j)
        scatter_in[pl.ds(me, 1), 0:sent_rows, :] = scatter_out[pl.ds(me, 1)]

        merged = jnp.zeros((rows_day * cats, LANES), f32)
        for t in near:
            b = block_of(t)
            for h in range(per_block):
                receive(scatter, b * per_block + h)
            arrived = scatter_in[pl.ds(b * per_block, per_block)].reshape(per_block * LANES, LANES)
            both = jnp.dot(place[b], jnp.concatenate(split(arrived), axis=1).astype(bf16),
                           preferred_element_type=f32)
            merged = merged + both[:, :LANES] + both[:, LANES:]
        pooled = [merged[row * cats:(row + 1) * cats] for row in range(rows_day)]
        dates = [date_pack[row:row + 1, :] for row in range(rows_day)]
        cat = cat_goal
        for _ in range(INNER):
            below = pooled[0] * dates[0]
            for row in range(1, rows_day):
                below = below + pooled[row] * dates[row]
            total = below
            for g in range(1, per_block):
                total = total + roll(below, g)
            cat = cat_goal / total
            dates = [date_goal[row:row + 1] / jnp.sum(cat * pooled[row], axis=0, keepdims=True)
                     for row in range(rows_day)]
        for row in range(rows_day):
            date_pack[row:row + 1, :] = dates[row]
        return cat, dates

    def merge_groups(parts):
        total = parts[0]
        for g in range(1, per_block):
            total = jnp.where(lane_group(total.shape[0]) == g, parts[g], total)
        return total

    def one_round(index, carry):
        cat, dates = fit(index)
        both = jnp.dot(select[...], jnp.concatenate(split(cat), axis=1).astype(bf16), preferred_element_type=f32)
        picked = both[:, :LANES] + both[:, LANES:]
        for j in range(n_item):
            at = [(j * per_block + g) * rows_select for g in range(per_block)]
            packed = merge_groups([picked[i:i + rows_select] for i in at])
            part_out[j, 0:rows_part, :] = packed[:rows_part]
            for row in range(rows_day):
                part_out[j, rows_part + row:rows_part + row + 1, :] = dates[row]
        for t in reversed(near):
            for h in range(per_block):
                send(part, block_of(t) * per_block + h)
        part_in[pl.ds(me, 1)] = part_out[pl.ds(me, 1)]
        sums = jnp.zeros((2 * local, items), f32)
        for t in near:
            b = block_of(t)
            for h in range(per_block):
                receive(part, b * per_block + h)
            sources = [part_in[b * per_block + h] for h in range(per_block)]
            for g in range(per_block):
                rows = unpack(sources, g)
                chosen_all[b, g * rows_part:(g + 1) * rows_part, :] = rows[:rows_part]
                date_all[b, g * rows_day:(g + 1) * rows_day, :] = rows[rows_part:rows_part + rows_day]
            sums = sums + block_sums(b)
        send_rows(index + 1, sums)
        sent(scatter)
        sent(part)
        return carry

    lax.fori_loop(0, ROUNDS - 1, one_round, 0)

    cat, dates = fit(ROUNDS - 1)
    solved_out[0:rows_cat, :] = merge_groups([cat[g * rows_cat:(g + 1) * rows_cat] for g in range(per_block)])
    for row in range(rows_day):
        solved_out[rows_cat + row:rows_cat + row + 1, :] = dates[row]
    for t in reversed(near):
        for h in range(per_block):
            send(solved, block_of(t) * per_block + h)
    solved_in[pl.ds(me, 1)] = solved_out[...][None]
    full = (group_ref[...] == lax.broadcasted_iota(jnp.int32, (items, items), 0)).astype(f32)
    by_cat = full.T[:, :cats].astype(bf16)
    factor_column = jnp.broadcast_to(factor_ref[...], (items, items)).T
    for t in near:
        b = block_of(t)
        for h in range(per_block):
            receive(solved, b * per_block + h)
        sources = [solved_in[b * per_block + h] for h in range(per_block)]
        at = pl.ds(pl.multiple_of(b * LANES, LANES), LANES)
        for g in range(per_block):
            rows = unpack(sources, g)
            cat_all[g * rows_cat:(g + 1) * rows_cat, :] = rows[:rows_cat]
            date_all[b, g * rows_day:(g + 1) * rows_day, :] = rows[rows_cat:rows_cat + rows_day]
        cat_ref[:, at] = cat_all[0:cats, :]
        date = date_all[b]
        date_ref[:, at] = date
        high, low = split(cat_all[...])
        spread = jnp.dot(by_cat, jnp.concatenate([high, low], axis=1).astype(bf16), preferred_element_type=f32)
        scaled = (spread[:, :LANES] + spread[:, LANES:]) * factor_column
        for d in range(days):
            out_ref[d, :, at] = (x_ref[d, :, at].astype(f32) * scaled * date[d:d + 1, :]).astype(bf16)
    sent(scatter)
    sent(solved)
    for index in range(ROUNDS):
        for off in range(1, n_store):
            row_copy(index, off, False).wait_send()


def shards(n_item, n_store, predicted_units, product_group, product_goal, group_outlet_goal, outlet_date_goal):
    items, days, stores = predicted_units.shape
    cats = group_outlet_goal.shape[0]
    least = max(1, items * n_item // (2 * cats))
    sent_cats = min(cats, (items - 2) // least + 2)
    per_block = LANES // (stores // n_item)
    rows_day = days // per_block
    rows_part = up(sent_cats, per_block) // per_block
    local = up(rows_part * per_block, 8)
    blocks = stores // LANES
    sent_rows = up(rows_day * sent_cats, 8)
    part_rows = up(rows_part + rows_day, 8)
    solved_rows = up(cats // per_block + rows_day, 8)
    f32 = jnp.float32
    vmem = pl.BlockSpec(memory_space=pltpu.VMEM)
    dma = pltpu.SemaphoreType.DMA
    factor, cat, date, out = pl.pallas_call(
        functools.partial(kernel, n_item, n_store, sent_cats),
        out_shape=(
            jax.ShapeDtypeStruct((1, items), f32),
            jax.ShapeDtypeStruct((cats, stores), f32),
            jax.ShapeDtypeStruct((days, stores), f32),
            jax.ShapeDtypeStruct((days, items, stores), jnp.bfloat16),
        ),
        in_specs=[vmem] * 6,
        out_specs=(vmem,) * 4,
        scratch_shapes=[
            pltpu.VMEM((blocks, local, LANES), f32),
            pltpu.VMEM((blocks, days, LANES), f32),
            pltpu.VMEM((cats, LANES), f32),
            pltpu.VMEM((n_item, sent_rows, LANES), f32),
            pltpu.VMEM((n_item, LANES, LANES), f32),
            pltpu.VMEM((n_item, part_rows, LANES), f32),
            pltpu.VMEM((n_item, part_rows, LANES), f32),
            pltpu.VMEM((solved_rows, LANES), f32),
            pltpu.VMEM((n_item, solved_rows, LANES), f32),
            pltpu.VMEM((up(rows_day, 8), LANES), f32),
            pltpu.VMEM((blocks, rows_day * cats, per_block * LANES), jnp.bfloat16),
            pltpu.VMEM((n_item * per_block * up(rows_part, 8), cats), jnp.bfloat16),
            pltpu.VMEM((ROUNDS, 8, items), f32),
            pltpu.VMEM((ROUNDS, n_store, 8, items), f32),
            pltpu.VMEM((8, LANES), f32),
            pltpu.VMEM((n_item, 8, LANES), f32),
            dma((n_item,)), dma((n_item,)), dma((n_item,)), dma((n_item,)), dma((n_item,)), dma((n_item,)),
            dma((ROUNDS, n_store)), dma((ROUNDS, n_store)), dma((n_item,)), dma((n_item,)),
        ],
        compiler_params=pltpu.CompilerParams(
            collective_id=0, has_side_effects=True, vmem_limit_bytes=40 * 1024 * 1024),
    )(predicted_units.transpose(1, 0, 2), product_group[None],
      jnp.broadcast_to(product_group[:1], (1, items)), product_goal[None], group_outlet_goal, outlet_date_goal)
    return factor[0], cat, date, out.transpose(1, 0, 2)


def solution(mesh):
    in_specs = (P("item", None, "store"), P("item"), P("item"), P(None, "store"), P(None, "store"))
    out_specs = (P("item"), P(None, "store"), P(None, "store"), P("item", None, "store"))
    body = functools.partial(shards, mesh.shape["item"], mesh.shape["store"])
    return jax.shard_map(body, mesh=mesh, in_specs=in_specs, out_specs=out_specs, check_vma=False)
```

time: 89.9 us -> 81.5 us (0.907)
  Pallas kernels: 83.5 us -> 74.4 us
    pallas_call x1, Pallas kernels: 83.5 us -> 74.4 us  [shards(): pl.pallas_call(functools.partial(kernel, n_item, n_store, sent_cats), out...]
where the time goes in v2:
time: 81.5 us; the launch traced here: 81.3 us
  Pallas kernels  74.4 us (91%)
  local copies, waits for them, and re-layouts  6.22 us (8%)
    pallas_call x1, Pallas kernels, shards(): pl.pallas_call(functools.partial(kernel, n_item, n_store, sent_cats), out...  74.4 us
    unnamed x13, local copies, waits for them, and re-layouts  6.18 us

profile of v2, /device:TPU:0, one launch (start us, length us, event | category | flops | bytes accessed | tf_op | source)
XLA Modules:
  0.0 81.3 jit_solution(453042670176245990)
XLA Ops:
  0.6 0.0 copy-start.2
  0.6 0.6 copy-done.2
  1.3 0.0 copy-start
  1.3 0.0 copy-start.1
  1.4 1.6 %copy.12 = bf16[128,8,512]{2,0,1:T(8,128)(2,1)S(1)} copy(bf16[128,8,512]{2,1,0:T(8,128)(2,1)} %param.5) | data formatting | bytes 2097152 | tf_op args[0]
  2.9 0.0 copy-start.3
  2.9 0.0 copy-done
  3.0 0.0 copy-done.1
  3.0 0.6 copy-done.3
  3.6 74.4 %shard_map.84 = (f32[1,128]{1,0:T(1,128)S(1)}, f32[64,512]{1,0:T(8,128)S(1)}, f32[8,512]{1,0:T(8,128)S(1)}, bf16[8,128,512]{2,1,0:T(8,128)(2,1)S(1)}) custom-call(bf16[8,128,512]{2,1,0:T(8,128)(2,1)S(1)} %bitcast.9, s32[1,128]{1,0:T(1,128)S(1)} %bitcast.12, s32[1,128]{1,0:T(1,128)S(1)} %broadcast_in_dim.12.first_ref, f32[1,128]{1,0:T(1,128)S(1)} %bitcast.13, ...), custom_call_target="tpu_custom_call" | custom-call | tf_op jit(solution)/shard_map/pallas_call | solution.py:315
  78.0 1.5 %copy.10 = bf16[128,8,512]{2,1,0:T(8,128)(2,1)} copy(bf16[128,8,512]{2,0,1:T(8,128)(2,1)S(1)} %bitcast.10) | data formatting | bytes 2097152
  79.5 0.5 copy.16
  80.0 0.7 copy.17
  80.7 0.6 copy.18
  (1 shorter events, 0.0 us)
Async XLA Ops:
  0.6 0.7 copy-start.2
  1.3 1.6 %copy-start = (f32[64,512]{1,0:T(8,128)S(1)}, f32[64,512]{1,0:T(8,128)}, u32[]{:S(2)}) copy-start(f32[64,512]{1,0:T(8,128)} %cat_goal_ref.1) | copy-start | bytes 393220
  1.3 1.6 %copy-start.1 = (f32[8,512]{1,0:T(8,128)S(1)}, f32[8,512]{1,0:T(8,128)}, u32[]{:S(2)}) copy-start(f32[8,512]{1,0:T(8,128)} %date_goal_ref.1) | copy-start | bytes 49156
  2.9 0.7 copy-start.3

commit v3 on v2

--- a/solution.py
+++ b/solution.py
@@ -22,8 +22,9 @@
     return high, value - high
 
 
-def kernel(n_item, n_store, sent_cats, x_ref, group_ref, first_ref, goal_ref, cat_goal_ref, date_goal_ref,
-           factor_ref, cat_ref, date_ref, out_ref,
+def kernel(n_item, n_store, sent_cats, x_hbm, cat_goal_hbm, date_goal_hbm, group_ref, first_ref, goal_ref,
+           factor_ref, cat_ref, date_ref, scale_ref,
+           x_raw, x_wide, x_ref, cat_goal_ref, date_goal_ref, local_sem,
            chosen_all, date_all, cat_all, scatter_out, scatter_in, part_out, part_in, solved_out, solved_in,
            date_pack, place, select, row_out, row_in, meta_out, meta_in,
            scatter_ssem, scatter_rsem, part_ssem, part_rsem, solved_ssem, solved_rsem,
@@ -45,6 +46,11 @@
     near = sorted(range(blocks), key=lambda t: (min(t, blocks - t), t))
     f32, bf16 = jnp.float32, jnp.bfloat16
 
+    local_copies = [
+        pltpu.make_async_copy(src, dst, local_sem.at[i])
+        for i, (src, dst) in enumerate(((x_hbm, x_raw), (cat_goal_hbm, cat_goal_ref), (date_goal_hbm, date_goal_ref)))]
+    for copy in local_copies:
+        copy.start()
     barrier = pltpu.get_barrier_semaphore()
     for off in range(1, n_item):
         pl.semaphore_signal(barrier, inc=1, device_id={"item": lax.rem(me + off, n_item)}, device_id_type=MESH)
@@ -131,6 +137,12 @@
     chosen_all[...] = jnp.ones(chosen_all.shape, f32)
     date_all[...] = jnp.ones(date_all.shape, f32)
     date_pack[...] = jnp.ones(date_pack.shape, f32)
+    local_copies[0].wait()
+    for b in range(blocks):
+        at = slice(b * LANES, (b + 1) * LANES)
+        x_wide[b] = x_raw[:, :, at].astype(f32).reshape(items * days, LANES)
+        for d in range(days):
+            x_ref[d, :, at] = x_wide[b, pl.ds(d, items, stride=days), :].astype(bf16)
     sums = block_sums(0)
     for b in range(1, blocks):
         sums = sums + block_sums(b)
@@ -139,6 +151,8 @@
         send(meta, lax.rem(me + off, n_item))
     send_rows(0, sums)
 
+    for copy in local_copies[1:]:
+        copy.wait()
     block_at = pl.multiple_of(my_block * LANES, LANES)
     group_at = lax.rem(me, per_block)
     cat_goal_all = cat_goal_ref[:, pl.ds(block_at, LANES)]
@@ -286,14 +300,20 @@
         date_ref[:, at] = date
         high, low = split(cat_all[...])
         spread = jnp.dot(by_cat, jnp.concatenate([high, low], axis=1).astype(bf16), preferred_element_type=f32)
-        scaled = (spread[:, :LANES] + spread[:, LANES:]) * factor_column
-        for d in range(days):
-            out_ref[d, :, at] = (x_ref[d, :, at].astype(f32) * scaled * date[d:d + 1, :]).astype(bf16)
+        scale_ref[:, at] = (spread[:, :LANES] + spread[:, LANES:]) * factor_column
     sent(scatter)
     sent(solved)
     for index in range(ROUNDS):
         for off in range(1, n_store):
             row_copy(index, off, False).wait_send()
+
+
+def finish(x_ref, scale_ref, factor_in, cat_in, date_in, factor_ref, cat_ref, date_ref, out_ref):
+    value = x_ref[...].astype(jnp.float32) * scale_ref[...][:, None, :] * date_in[...][None]
+    out_ref[...] = value.astype(jnp.bfloat16)
+    factor_ref[...] = factor_in[...]
+    cat_ref[...] = cat_in[...]
+    date_ref[...] = date_in[...]
 
 
 def shards(n_item, n_store, predicted_units, product_group, product_goal, group_outlet_goal, outlet_date_goal):
@@ -312,17 +332,24 @@
     f32 = jnp.float32
     vmem = pl.BlockSpec(memory_space=pltpu.VMEM)
     dma = pltpu.SemaphoreType.DMA
-    factor, cat, date, out = pl.pallas_call(
+    anywhere = pl.BlockSpec(memory_space=pl.ANY)
+    factor, cat, date, scale = pl.pallas_call(
         functools.partial(kernel, n_item, n_store, sent_cats),
         out_shape=(
             jax.ShapeDtypeStruct((1, items), f32),
             jax.ShapeDtypeStruct((cats, stores), f32),
             jax.ShapeDtypeStruct((days, stores), f32),
-            jax.ShapeDtypeStruct((days, items, stores), jnp.bfloat16),
+            jax.ShapeDtypeStruct((items, stores), f32),
         ),
-        in_specs=[vmem] * 6,
+        in_specs=[anywhere] * 3 + [vmem] * 3,
         out_specs=(vmem,) * 4,
         scratch_shapes=[
+            pltpu.VMEM((items, days, stores), jnp.bfloat16),
+            pltpu.VMEM((blocks, items * days, LANES), f32),
+            pltpu.VMEM((days, items, stores), jnp.bfloat16),
+            pltpu.VMEM((cats, stores), f32),
+            pltpu.VMEM((days, stores), f32),
+            dma((3,)),
             pltpu.VMEM((blocks, local, LANES), f32),
             pltpu.VMEM((blocks, days, LANES), f32),
             pltpu.VMEM((cats, LANES), f32),
@@ -344,9 +371,31 @@
         ],
         compiler_params=pltpu.CompilerParams(
             collective_id=0, has_side_effects=True, vmem_limit_bytes=40 * 1024 * 1024),
-    )(predicted_units.transpose(1, 0, 2), product_group[None],
-      jnp.broadcast_to(product_group[:1], (1, items)), product_goal[None], group_outlet_goal, outlet_date_goal)
-    return factor[0], cat, date, out.transpose(1, 0, 2)
+    )(predicted_units, group_outlet_goal, outlet_date_goal, product_group[None],
+      jnp.broadcast_to(product_group[:1], (1, items)), product_goal[None])
+    steps = 4
+    part = items // steps
+    same = lambda shape: pl.BlockSpec(shape, lambda i: (0,) * len(shape))
+    factor, cat, date, out = pl.pallas_call(
+        finish,
+        grid=(steps,),
+        out_shape=(
+            jax.ShapeDtypeStruct((1, items), f32),
+            jax.ShapeDtypeStruct((cats, stores), f32),
+            jax.ShapeDtypeStruct((days, stores), f32),
+            jax.ShapeDtypeStruct((items, days, stores), jnp.bfloat16),
+        ),
+        in_specs=[
+            pl.BlockSpec((part, days, stores), lambda i: (i, 0, 0)),
+            pl.BlockSpec((part, stores), lambda i: (i, 0)),
+            same((1, items)), same((cats, stores)), same((days, stores)),
+        ],
+        out_specs=(
+            same((1, items)), same((cats, stores)), same((days, stores)),
+            pl.BlockSpec((part, days, stores), lambda i: (i, 0, 0)),
+        ),
+    )(predicted_units, scale, factor, cat, date)
+    return factor[0], cat, date, out
 
 
 def solution(mesh):

time: 81.5 us -> 86 us (1.055)
  Pallas kernels: 74.4 us -> 78.4 us
    pallas_call x0 -> x1, Pallas kernels: none -> 3.59 us  [shards(): pl.pallas_call(finish, grid=(steps,), out_shape=(jax.ShapeDtypeStruct((1,...]
    unnamed x13 -> x18, local copies, waits for them, and re-layouts: 6.18 us -> 6.56 us
where the time goes in v3:
time: 86 us; the launch traced here: 85.7 us
  Pallas kernels  78.4 us (91%)
  local copies, waits for them, and re-layouts  6.6 us (8%)
    pallas_call x1, Pallas kernels, shards(): pl.pallas_call(functools.partial(kernel, n_item, n_store, sent_cats), out...  74.8 us
    unnamed x18, local copies, waits for them, and re-layouts  6.56 us
    pallas_call x1, Pallas kernels, shards(): pl.pallas_call(finish, grid=(steps,), out_shape=(jax.ShapeDtypeStruct((1,...  3.59 us

profile of v3, /device:TPU:0, one launch (start us, length us, event | category | flops | bytes accessed | tf_op | source)
XLA Modules:
  0.0 85.7 jit_solution(15203567624983119809)
XLA Ops:
  0.6 0.0 copy-start.6
  0.6 0.6 copy-done.6
  1.3 0.0 copy-start.7
  1.3 0.6 copy-done.7
  1.9 0.0 copy-start
  1.9 1.2 %copy-done = bf16[128,8,512]{2,1,0:T(8,128)(2,1)S(1)} copy-done((bf16[128,8,512]{2,1,0:T(8,128)(2,1)S(1)}, bf16[128,8,512]{2,1,0:T(8,128)(2,1)}, u32[]{:S(2)}) %copy-start) | copy-done | bytes 1048600
  3.2 0.0 copy-start.2
  3.2 0.9 %copy-done.2 = f32[64,512]{1,0:T(8,128)S(1)} copy-done((f32[64,512]{1,0:T(8,128)S(1)}, f32[64,512]{1,0:T(8,128)}, u32[]{:S(2)}) %copy-start.2) | copy-done | bytes 131096
  4.1 0.0 copy-start.4
  4.1 0.7 copy-done.4
  4.8 74.8 %shard_map.84 = (f32[1,128]{1,0:T(1,128)S(1)}, f32[64,512]{1,0:T(8,128)S(1)}, f32[8,512]{1,0:T(8,128)S(1)}, f32[128,512]{1,0:T(8,128)S(1)}) custom-call(bf16[128,8,512]{2,1,0:T(8,128)(2,1)S(1)} %copy-done, f32[64,512]{1,0:T(8,128)S(1)} %copy-done.2, f32[8,512]{1,0:T(8,128)S(1)} %copy-done.4, s32[1,128]{1,0:T(1,128)S(1)} %bitcast.6, ...), custom_call_target="tpu_custom_call" | custom-call | tf_op jit(solution)/shard_map/pallas_call | solution.py:336
  79.6 0.0 copy-start.1
  79.6 0.7 copy-done.1
  80.3 0.0 copy-start.3
  80.3 0.7 copy-done.3
  81.0 0.0 copy-start.5
  81.0 0.6 copy-done.5
  81.6 0.0 copy-start.8
  81.6 0.5 copy-done.8
  82.1 3.6 %shard_map.85 = (f32[1,128]{1,0:T(1,128)}, f32[64,512]{1,0:T(8,128)}, f32[8,512]{1,0:T(8,128)}, bf16[128,8,512]{2,1,0:T(8,128)(2,1)}) custom-call(bf16[128,8,512]{2,1,0:T(8,128)(2,1)} %x_ref.1, f32[128,512]{1,0:T(8,128)} %copy-done.1, f32[1,128]{1,0:T(1,128)} %copy-done.8, f32[64,512]{1,0:T(8,128)} %copy-done.3, f32[8,512]{1,0:T(8,128)} %copy-done.5), custom_call_target="tpu_custom_call" | custom-call | tf_op jit(solution)/shard_map/pallas_call | solution.py:379
  (1 shorter events, 0.0 us)
Async XLA Ops:
  0.6 0.7 copy-start.6
  1.3 0.7 copy-start.7
  1.9 1.2 %copy-start = (bf16[128,8,512]{2,1,0:T(8,128)(2,1)S(1)}, bf16[128,8,512]{2,1,0:T(8,128)(2,1)}, u32[]{:S(2)}) copy-start(bf16[128,8,512]{2,1,0:T(8,128)(2,1)} %x_ref.1) | copy-start | bytes 3145732
  3.2 0.9 %copy-start.2 = (f32[64,512]{1,0:T(8,128)S(1)}, f32[64,512]{1,0:T(8,128)}, u32[]{:S(2)}) copy-start(f32[64,512]{1,0:T(8,128)} %cat_goal_hbm.1) | copy-start | bytes 393220
  4.1 0.7 copy-start.4
  79.6 0.7 copy-start.1
  80.3 0.7 copy-start.3
  81.0 0.6 copy-start.5
  81.6 0.5 copy-start.8

commit v4 on v3

--- a/solution.py
+++ b/solution.py
@@ -10,6 +10,7 @@
 ROUNDS = 4
 INNER = 3
 LANES = 128
+VMEM_BYTES = 60 * 1024 * 1024
 MESH = pl.DeviceIdType.MESH
 
 
@@ -22,9 +23,9 @@
     return high, value - high
 
 
-def kernel(n_item, n_store, sent_cats, x_hbm, cat_goal_hbm, date_goal_hbm, group_ref, first_ref, goal_ref,
+def kernel(n_item, n_store, sent_cats, x_hbm, group_hbm, goal_hbm, cat_goal_hbm, date_goal_hbm,
            factor_ref, cat_ref, date_ref, scale_ref,
-           x_raw, x_wide, x_ref, cat_goal_ref, date_goal_ref, local_sem,
+           x_raw, x_wide, x_ref, group_ref, goal_ref, cat_goal_ref, date_goal_ref, local_sem,
            chosen_all, date_all, cat_all, scatter_out, scatter_in, part_out, part_in, solved_out, solved_in,
            date_pack, place, select, row_out, row_in, meta_out, meta_in,
            scatter_ssem, scatter_rsem, part_ssem, part_rsem, solved_ssem, solved_rsem,
@@ -43,12 +44,13 @@
     me = lax.axis_index("item")
     mine = lax.axis_index("store")
     my_block = me // per_block
+    group_at = lax.rem(me, per_block)
     near = sorted(range(blocks), key=lambda t: (min(t, blocks - t), t))
     f32, bf16 = jnp.float32, jnp.bfloat16
 
-    local_copies = [
-        pltpu.make_async_copy(src, dst, local_sem.at[i])
-        for i, (src, dst) in enumerate(((x_hbm, x_raw), (cat_goal_hbm, cat_goal_ref), (date_goal_hbm, date_goal_ref)))]
+    moves = ((x_hbm, x_raw), (group_hbm, group_ref), (goal_hbm, goal_ref),
+             (cat_goal_hbm, cat_goal_ref), (date_goal_hbm, date_goal_ref))
+    local_copies = [pltpu.make_async_copy(src, dst, local_sem.at[i]) for i, (src, dst) in enumerate(moves)]
     for copy in local_copies:
         copy.start()
     barrier = pltpu.get_barrier_semaphore()
@@ -82,11 +84,13 @@
             src_ref=src(peer), dst_ref=dst(slot), send_sem=ssem.at[peer], recv_sem=rsem.at[slot],
             device_id={"item": peer}, device_id_type=MESH)
 
-    def send(kind, peer):
-        pl.when(peer != me)(lambda: item_copy(kind, peer, False).start())
-
-    def receive(kind, peer):
-        pl.when(peer != me)(lambda: item_copy(kind, peer, True).wait_recv())
+    def send(kind, t):
+        for peer in peers_of(t):
+            item_copy(kind, peer, False).start()
+
+    def receive(kind, t):
+        for peer in peers_of(t):
+            item_copy(kind, peer, True).wait_recv()
 
     def sent(kind):
         for off in range(1, n_item):
@@ -94,6 +98,12 @@
 
     def block_of(t):
         return lax.rem(my_block + t, blocks)
+
+    def peers_of(t):
+        base = block_of(t) * per_block
+        if t:
+            return [base + h for h in range(per_block)]
+        return [base + lax.rem(group_at + off, per_block) for off in range(1, per_block)]
 
     meta = (lambda j: meta_out, lambda j: meta_in.at[j], meta_ssem, meta_rsem)
     scatter = (lambda j: scatter_out.at[j], lambda j: scatter_in.at[j, pl.ds(0, sent_rows)], scatter_ssem, scatter_rsem)
@@ -108,7 +118,8 @@
             send_sem=row_ssem.at[index, peer], recv_sem=row_rsem.at[index, slot],
             device_id={"store": peer}, device_id_type=MESH)
 
-    first = first_ref[...]
+    local_copies[1].wait()
+    first = jnp.min(group_ref[...], axis=1, keepdims=True)
     onehot = (group_ref[...] - first == lax.broadcasted_iota(jnp.int32, (local, items), 0)).astype(f32)
 
     def x_block(b, axis):
@@ -128,7 +139,7 @@
             row_copy(index, off, False).start()
         row_in[index, mine] = jnp.broadcast_to(row_sum, (8, items))
 
-    meta_out[...] = jnp.broadcast_to(first.astype(f32), meta_out.shape)
+    meta_out[...] = jnp.broadcast_to(first, meta_out.shape).astype(f32)
     meta_in[pl.ds(me, 1)] = meta_out[...][None]
     scatter_in[...] = jnp.zeros(scatter_in.shape, f32)
     scatter_out[...] = jnp.zeros(scatter_out.shape, f32)
@@ -147,14 +158,13 @@
     for b in range(1, blocks):
         sums = sums + block_sums(b)
     pl.semaphore_wait(barrier, n_item + n_store - 2)
-    for off in range(1, n_item):
-        send(meta, lax.rem(me + off, n_item))
+    for t in reversed(near):
+        send(meta, t)
     send_rows(0, sums)
 
-    for copy in local_copies[1:]:
+    for copy in local_copies[2:]:
         copy.wait()
     block_at = pl.multiple_of(my_block * LANES, LANES)
-    group_at = lax.rem(me, per_block)
     cat_goal_all = cat_goal_ref[:, pl.ds(block_at, LANES)]
     date_goal_all = date_goal_ref[:, pl.ds(block_at, LANES)]
     cat_goal = jnp.zeros((cats, LANES), f32)
@@ -165,8 +175,8 @@
         date_parts = [date_goal_all[g * rows_day:(g + 1) * rows_day] for g in range(per_block)]
         date_goal = jnp.where(here, pack(date_parts, h), date_goal)
 
-    for off in range(1, n_item):
-        receive(meta, lax.rem(me + off, n_item))
+    for t in near:
+        receive(meta, t)
     sent(meta)
     row_index = lax.broadcasted_iota(jnp.int32, (rows_day * cats, LANES), 0)
     lane_index = lax.broadcasted_iota(jnp.int32, (rows_day * cats, LANES), 1)
@@ -207,14 +217,13 @@
                     at = [(g * rows_day + row) * LANES for g in range(per_block)]
                     packed = pack([pool[:, i:i + LANES] for i in at], h)
                     scatter_out[j, row * sent_cats:(row + 1) * sent_cats, :] = packed[:sent_cats]
-                send(scatter, j)
+            send(scatter, t)
         scatter_in[pl.ds(me, 1), 0:sent_rows, :] = scatter_out[pl.ds(me, 1)]
 
         merged = jnp.zeros((rows_day * cats, LANES), f32)
         for t in near:
             b = block_of(t)
-            for h in range(per_block):
-                receive(scatter, b * per_block + h)
+            receive(scatter, t)
             arrived = scatter_in[pl.ds(b * per_block, per_block)].reshape(per_block * LANES, LANES)
             both = jnp.dot(place[b], jnp.concatenate(split(arrived), axis=1).astype(bf16),
                            preferred_element_type=f32)
@@ -253,14 +262,12 @@
             for row in range(rows_day):
                 part_out[j, rows_part + row:rows_part + row + 1, :] = dates[row]
         for t in reversed(near):
-            for h in range(per_block):
-                send(part, block_of(t) * per_block + h)
+            send(part, t)
         part_in[pl.ds(me, 1)] = part_out[pl.ds(me, 1)]
         sums = jnp.zeros((2 * local, items), f32)
         for t in near:
             b = block_of(t)
-            for h in range(per_block):
-                receive(part, b * per_block + h)
+            receive(part, t)
             sources = [part_in[b * per_block + h] for h in range(per_block)]
             for g in range(per_block):
                 rows = unpack(sources, g)
@@ -279,16 +286,14 @@
     for row in range(rows_day):
         solved_out[rows_cat + row:rows_cat + row + 1, :] = dates[row]
     for t in reversed(near):
-        for h in range(per_block):
-            send(solved, block_of(t) * per_block + h)
+        send(solved, t)
     solved_in[pl.ds(me, 1)] = solved_out[...][None]
     full = (group_ref[...] == lax.broadcasted_iota(jnp.int32, (items, items), 0)).astype(f32)
     by_cat = full.T[:, :cats].astype(bf16)
     factor_column = jnp.broadcast_to(factor_ref[...], (items, items)).T
     for t in near:
         b = block_of(t)
-        for h in range(per_block):
-            receive(solved, b * per_block + h)
+        receive(solved, t)
         sources = [solved_in[b * per_block + h] for h in range(per_block)]
         at = pl.ds(pl.multiple_of(b * LANES, LANES), LANES)
         for g in range(per_block):
@@ -309,8 +314,10 @@
 
 
 def finish(x_ref, scale_ref, factor_in, cat_in, date_in, factor_ref, cat_ref, date_ref, out_ref):
-    value = x_ref[...].astype(jnp.float32) * scale_ref[...][:, None, :] * date_in[...][None]
-    out_ref[...] = value.astype(jnp.bfloat16)
+    date = date_in[...]
+    for i in range(x_ref.shape[0]):
+        value = x_ref[i].astype(jnp.float32) * (scale_ref[i:i + 1, :] * date)
+        out_ref[i] = value.astype(jnp.bfloat16)
     factor_ref[...] = factor_in[...]
     cat_ref[...] = cat_in[...]
     date_ref[...] = date_in[...]
@@ -341,15 +348,17 @@
             jax.ShapeDtypeStruct((days, stores), f32),
             jax.ShapeDtypeStruct((items, stores), f32),
         ),
-        in_specs=[anywhere] * 3 + [vmem] * 3,
+        in_specs=[anywhere] * 5,
         out_specs=(vmem,) * 4,
         scratch_shapes=[
             pltpu.VMEM((items, days, stores), jnp.bfloat16),
             pltpu.VMEM((blocks, items * days, LANES), f32),
             pltpu.VMEM((days, items, stores), jnp.bfloat16),
+            pltpu.VMEM((1, items), jnp.int32),
+            pltpu.VMEM((1, items), f32),
             pltpu.VMEM((cats, stores), f32),
             pltpu.VMEM((days, stores), f32),
-            dma((3,)),
+            dma((5,)),
             pltpu.VMEM((blocks, local, LANES), f32),
             pltpu.VMEM((blocks, days, LANES), f32),
             pltpu.VMEM((cats, LANES), f32),
@@ -370,9 +379,8 @@
             dma((ROUNDS, n_store)), dma((ROUNDS, n_store)), dma((n_item,)), dma((n_item,)),
         ],
         compiler_params=pltpu.CompilerParams(
-            collective_id=0, has_side_effects=True, vmem_limit_bytes=40 * 1024 * 1024),
-    )(predicted_units, group_outlet_goal, outlet_date_goal, product_group[None],
-      jnp.broadcast_to(product_group[:1], (1, items)), product_goal[None])
+            collective_id=0, has_side_effects=True, vmem_limit_bytes=VMEM_BYTES),
+    )(predicted_units, product_group[None], product_goal[None], group_outlet_goal, outlet_date_goal)
     steps = 4
     part = items // steps
     same = lambda shape: pl.BlockSpec(shape, lambda i: (0,) * len(shape))
@@ -394,6 +402,7 @@
             same((1, items)), same((cats, stores)), same((days, stores)),
             pl.BlockSpec((part, days, stores), lambda i: (i, 0, 0)),
         ),
+        compiler_params=pltpu.CompilerParams(vmem_limit_bytes=VMEM_BYTES),
     )(predicted_units, scale, factor, cat, date)
     return factor[0], cat, date, out
 

time: 86 us -> 79.9 us (0.929)
  local copies, waits for them, and re-layouts: 6.6 us -> 0 us
    unnamed x18 -> x0, local copies, waits for them, and re-layouts: 6.56 us -> none
where the time goes in v4:
time: 79.9 us; the launch traced here: 79.7 us
  Pallas kernels  79.1 us (99%)
    pallas_call x1, Pallas kernels, shards(): pl.pallas_call(functools.partial(kernel, n_item, n_store, sent_cats), out...  75.5 us
    pallas_call x1, Pallas kernels, shards(): pl.pallas_call(finish, grid=(steps,), out_shape=(jax.ShapeDtypeStruct((1,...  3.59 us

profile of v4, /device:TPU:0, one launch (start us, length us, event | category | flops | bytes accessed | tf_op | source)
XLA Modules:
  0.0 79.7 jit_solution(17619619166995114216)
XLA Ops:
  0.6 75.5 %shard_map.84 = (f32[1,128]{1,0:T(1,128)}, f32[64,512]{1,0:T(8,128)}, f32[8,512]{1,0:T(8,128)}, f32[128,512]{1,0:T(8,128)}) custom-call(bf16[128,8,512]{2,1,0:T(8,128)(2,1)} %x_ref.1, s32[1,128]{1,0:T(1,128)} %bitcast.3, f32[1,128]{1,0:T(1,128)} %bitcast.4, f32[64,512]{1,0:T(8,128)} %cat_goal_hbm.1, f32[8,512]{1,0:T(8,128)} %date_goal_hbm.1), custom_call_target="tpu_custom_call" | custom-call | tf_op jit(solution)/shard_map/pallas_call | solution.py:343
  76.1 3.6 %shard_map.85 = (f32[1,128]{1,0:T(1,128)}, f32[64,512]{1,0:T(8,128)}, f32[8,512]{1,0:T(8,128)}, bf16[128,8,512]{2,1,0:T(8,128)(2,1)}) custom-call(bf16[128,8,512]{2,1,0:T(8,128)(2,1)} %x_ref.1, f32[128,512]{1,0:T(8,128)} %get-tuple-element.12.scale_ref, f32[1,128]{1,0:T(1,128)} %get-tuple-element.13.factor_in, f32[64,512]{1,0:T(8,128)} %get-tuple-element.14.cat_in, ...), custom_call_target="tpu_custom_call" | custom-call | tf_op jit(solution)/shard_map/pallas_call | solution.py:387

commit v5 on v4

--- a/solution.py
+++ b/solution.py
@@ -25,12 +25,12 @@
 
 def kernel(n_item, n_store, sent_cats, x_hbm, group_hbm, goal_hbm, cat_goal_hbm, date_goal_hbm,
            factor_ref, cat_ref, date_ref, scale_ref,
-           x_raw, x_wide, x_ref, group_ref, goal_ref, cat_goal_ref, date_goal_ref, local_sem,
+           x_raw, x_wide, x_ref, x_turned, group_ref, goal_ref, cat_goal_ref, date_goal_ref, local_sem,
            chosen_all, date_all, cat_all, scatter_out, scatter_in, part_out, part_in, solved_out, solved_in,
            date_pack, place, select, row_out, row_in, meta_out, meta_in,
            scatter_ssem, scatter_rsem, part_ssem, part_rsem, solved_ssem, solved_rsem,
            row_ssem, row_rsem, meta_ssem, meta_rsem):
-    days, items, stores = x_ref.shape
+    items, days, stores = x_raw.shape
     cats = cat_goal_ref.shape[0]
     local = chosen_all.shape[1]
     chunk = stores // n_item
@@ -122,15 +122,13 @@
     first = jnp.min(group_ref[...], axis=1, keepdims=True)
     onehot = (group_ref[...] - first == lax.broadcasted_iota(jnp.int32, (local, items), 0)).astype(f32)
 
-    def x_block(b, axis):
-        at = pl.ds(pl.multiple_of(b * LANES, LANES), LANES)
-        return jnp.concatenate([x_ref[d, :, at] for d in range(days)], axis=axis)
-
-    def block_sums(b):
+    def block_sums(b, turned=True):
         chosen, date = chosen_all[b], date_all[b]
         high, low = split(jnp.concatenate([chosen * date[d:d + 1, :] for d in range(days)], axis=1))
         weight = jnp.concatenate([high, low], axis=0).astype(bf16)
-        return lax.dot_general(weight, x_block(b, 1), (((1,), (1,)), ((), ())), preferred_element_type=f32)
+        if turned:
+            return jnp.dot(weight, x_turned[b], preferred_element_type=f32)
+        return lax.dot_general(weight, x_ref[b], (((1,), (1,)), ((), ())), preferred_element_type=f32)
 
     def send_rows(index, sums):
         row_sum = jnp.sum(onehot * (sums[:local] + sums[local:]), axis=0, keepdims=True)
@@ -153,14 +151,18 @@
         at = slice(b * LANES, (b + 1) * LANES)
         x_wide[b] = x_raw[:, :, at].astype(f32).reshape(items * days, LANES)
         for d in range(days):
-            x_ref[d, :, at] = x_wide[b, pl.ds(d, items, stride=days), :].astype(bf16)
-    sums = block_sums(0)
+            x_ref[b, :, d * LANES:(d + 1) * LANES] = x_wide[b, pl.ds(d, items, stride=days), :].astype(bf16)
+    sums = block_sums(0, False)
     for b in range(1, blocks):
-        sums = sums + block_sums(b)
+        sums = sums + block_sums(b, False)
     pl.semaphore_wait(barrier, n_item + n_store - 2)
     for t in reversed(near):
         send(meta, t)
     send_rows(0, sums)
+    for b in range(blocks):
+        for d in range(days):
+            x_turned[b, d * LANES:(d + 1) * LANES, :] = (
+                x_wide[b, pl.ds(d, items, stride=days), :].T.astype(bf16))
 
     for copy in local_copies[2:]:
         copy.wait()
@@ -209,7 +211,7 @@
         weight = jnp.concatenate([high, low], axis=0).astype(bf16)
         for t in reversed(near):
             b = block_of(t)
-            both = jnp.dot(weight, x_block(b, 1), preferred_element_type=f32)
+            both = jnp.dot(weight, x_ref[b], preferred_element_type=f32)
             pool = both[:local] + both[local:]
             for h in range(per_block):
                 j = b * per_block + h
@@ -353,7 +355,8 @@
         scratch_shapes=[
             pltpu.VMEM((items, days, stores), jnp.bfloat16),
             pltpu.VMEM((blocks, items * days, LANES), f32),
-            pltpu.VMEM((days, items, stores), jnp.bfloat16),
+            pltpu.VMEM((blocks, items, days * LANES), jnp.bfloat16),
+            pltpu.VMEM((blocks, days * LANES, items), jnp.bfloat16),
             pltpu.VMEM((1, items), jnp.int32),
             pltpu.VMEM((1, items), f32),
             pltpu.VMEM((cats, stores), f32),
@@ -381,7 +384,7 @@
         compiler_params=pltpu.CompilerParams(
             collective_id=0, has_side_effects=True, vmem_limit_bytes=VMEM_BYTES),
     )(predicted_units, product_group[None], product_goal[None], group_outlet_goal, outlet_date_goal)
-    steps = 4
+    steps = 2
     part = items // steps
     same = lambda shape: pl.BlockSpec(shape, lambda i: (0,) * len(shape))
     factor, cat, date, out = pl.pallas_call(

time: 79.9 us -> 78.4 us (0.981)
  Pallas kernels: 79.1 us -> 77.6 us
    pallas_call x1, Pallas kernels: 3.59 us -> 2.28 us  [shards(): pl.pallas_call(finish, grid=(steps,), out_shape=(jax.ShapeDtypeStruct((1,...]
where the time goes in v5:
time: 78.4 us; the launch traced here: 78.2 us
  Pallas kernels  77.6 us (99%)
    pallas_call x1, Pallas kernels, shards(): pl.pallas_call(functools.partial(kernel, n_item, n_store, sent_cats), out...  75.3 us
    pallas_call x1, Pallas kernels, shards(): pl.pallas_call(finish, grid=(steps,), out_shape=(jax.ShapeDtypeStruct((1,...  2.28 us

profile of v5, /device:TPU:0, one launch (start us, length us, event | category | flops | bytes accessed | tf_op | source)
XLA Modules:
  0.0 78.2 jit_solution(14667758997871634279)
XLA Ops:
  0.6 75.3 %shard_map.84 = (f32[1,128]{1,0:T(1,128)}, f32[64,512]{1,0:T(8,128)}, f32[8,512]{1,0:T(8,128)}, f32[128,512]{1,0:T(8,128)}) custom-call(bf16[128,8,512]{2,1,0:T(8,128)(2,1)} %x_ref.1, s32[1,128]{1,0:T(1,128)} %bitcast.3, f32[1,128]{1,0:T(1,128)} %bitcast.4, f32[64,512]{1,0:T(8,128)} %cat_goal_hbm.1, f32[8,512]{1,0:T(8,128)} %date_goal_hbm.1), custom_call_target="tpu_custom_call" | custom-call | tf_op jit(solution)/shard_map/pallas_call | solution.py:345
  76.0 2.3 %shard_map.85 = (f32[1,128]{1,0:T(1,128)}, f32[64,512]{1,0:T(8,128)}, f32[8,512]{1,0:T(8,128)}, bf16[128,8,512]{2,1,0:T(8,128)(2,1)}) custom-call(bf16[128,8,512]{2,1,0:T(8,128)(2,1)} %x_ref.1, f32[128,512]{1,0:T(8,128)} %get-tuple-element.12.scale_ref, f32[1,128]{1,0:T(1,128)} %get-tuple-element.13.factor_in, f32[64,512]{1,0:T(8,128)} %get-tuple-element.14.cat_in, ...), custom_call_target="tpu_custom_call" | custom-call | tf_op jit(solution)/shard_map/pallas_call | solution.py:390

commit v6 on v5

--- a/solution.py
+++ b/solution.py
@@ -106,9 +106,10 @@
         return [base + lax.rem(group_at + off, per_block) for off in range(1, per_block)]
 
     meta = (lambda j: meta_out, lambda j: meta_in.at[j], meta_ssem, meta_rsem)
-    scatter = (lambda j: scatter_out.at[j], lambda j: scatter_in.at[j, pl.ds(0, sent_rows)], scatter_ssem, scatter_rsem)
-    part = (lambda j: part_out.at[j], lambda j: part_in.at[j], part_ssem, part_rsem)
-    solved = (lambda j: solved_out, lambda j: solved_in.at[j], solved_ssem, solved_rsem)
+    used = [pl.ds(0, n) for n in (rows_day * sent_cats, rows_part + rows_day, rows_cat + rows_day)]
+    scatter = (lambda j: scatter_out.at[j, used[0]], lambda j: scatter_in.at[j, used[0]], scatter_ssem, scatter_rsem)
+    part = (lambda j: part_out.at[j, used[1]], lambda j: part_in.at[j, used[1]], part_ssem, part_rsem)
+    solved = (lambda j: solved_out.at[used[2]], lambda j: solved_in.at[j, used[2]], solved_ssem, solved_rsem)
 
     def row_copy(index, off, arriving):
         peer = lax.rem(mine + off, n_store)
@@ -142,6 +143,8 @@
     scatter_in[...] = jnp.zeros(scatter_in.shape, f32)
     scatter_out[...] = jnp.zeros(scatter_out.shape, f32)
     part_out[...] = jnp.zeros(part_out.shape, f32)
+    part_in[...] = jnp.zeros(part_in.shape, f32)
+    solved_in[...] = jnp.zeros(solved_in.shape, f32)
     solved_out[...] = jnp.zeros(solved_out.shape, f32)
     chosen_all[...] = jnp.ones(chosen_all.shape, f32)
     date_all[...] = jnp.ones(date_all.shape, f32)
@@ -384,7 +387,7 @@
         compiler_params=pltpu.CompilerParams(
             collective_id=0, has_side_effects=True, vmem_limit_bytes=VMEM_BYTES),
     )(predicted_units, product_group[None], product_goal[None], group_outlet_goal, outlet_date_goal)
-    steps = 2
+    steps = 1
     part = items // steps
     same = lambda shape: pl.BlockSpec(shape, lambda i: (0,) * len(shape))
     factor, cat, date, out = pl.pallas_call(

time: 78.4 us -> 76.9 us (0.981)
  Pallas kernels: 77.6 us -> 76.1 us
    pallas_call x1, Pallas kernels: 75.3 us -> 73.5 us  [shards(): pl.pallas_call(functools.partial(kernel, n_item, n_store, sent_cats), out...]
where the time goes in v6:
time: 76.9 us; the launch traced here: 76.8 us
  Pallas kernels  76.1 us (99%)
    pallas_call x1, Pallas kernels, shards(): pl.pallas_call(functools.partial(kernel, n_item, n_store, sent_cats), out...  73.5 us
    pallas_call x1, Pallas kernels, shards(): pl.pallas_call(finish, grid=(steps,), out_shape=(jax.ShapeDtypeStruct((1,...  2.6 us

profile of v6, /device:TPU:0, one launch (start us, length us, event | category | flops | bytes accessed | tf_op | source)
XLA Modules:
  0.0 76.8 jit_solution(2188673091724499991)
XLA Ops:
  0.6 73.5 %shard_map.84 = (f32[1,128]{1,0:T(1,128)}, f32[64,512]{1,0:T(8,128)}, f32[8,512]{1,0:T(8,128)}, f32[128,512]{1,0:T(8,128)}) custom-call(bf16[128,8,512]{2,1,0:T(8,128)(2,1)} %x_ref.1, s32[1,128]{1,0:T(1,128)} %bitcast.3, f32[1,128]{1,0:T(1,128)} %bitcast.4, f32[64,512]{1,0:T(8,128)} %cat_goal_hbm.1, f32[8,512]{1,0:T(8,128)} %date_goal_hbm.1), custom_call_target="tpu_custom_call" | custom-call | tf_op jit(solution)/shard_map/pallas_call | solution.py:348
  74.2 2.6 %shard_map.85 = (f32[1,128]{1,0:T(1,128)}, f32[64,512]{1,0:T(8,128)}, f32[8,512]{1,0:T(8,128)}, bf16[128,8,512]{2,1,0:T(8,128)(2,1)}) custom-call(bf16[128,8,512]{2,1,0:T(8,128)(2,1)} %x_ref.1, f32[128,512]{1,0:T(8,128)} %get-tuple-element.12.scale_ref, f32[1,128]{1,0:T(1,128)} %get-tuple-element.13.factor_in, f32[64,512]{1,0:T(8,128)} %get-tuple-element.14.cat_in, ...), custom_call_target="tpu_custom_call" | custom-call | tf_op jit(solution)/shard_map/pallas_call | solution.py:393

commit v7 on v6

--- a/solution.py
+++ b/solution.py
@@ -115,7 +115,7 @@
         peer = lax.rem(mine + off, n_store)
         slot = peer if arriving else mine
         return pltpu.make_async_remote_copy(
-            src_ref=row_out.at[index], dst_ref=row_in.at[index, slot],
+            src_ref=row_out.at[index, pl.ds(0, 1)], dst_ref=row_in.at[index, slot, pl.ds(0, 1)],
             send_sem=row_ssem.at[index, peer], recv_sem=row_rsem.at[index, slot],
             device_id={"store": peer}, device_id_type=MESH)
 
@@ -204,10 +204,10 @@
     def fit(index):
         for off in range(1, n_store):
             row_copy(index, off, True).wait_recv()
-        whole = row_in[index, 0]
+        whole = row_in[index, 0, 0:1]
         for t in range(1, n_store):
-            whole = whole + row_in[index, t]
-        factor = goal_ref[...] / whole[0:1, :]
+            whole = whole + row_in[index, t, 0:1]
+        factor = goal_ref[...] / whole
         factor_ref[...] = factor
 
         high, low = split(onehot * factor)
@@ -387,7 +387,7 @@
         compiler_params=pltpu.CompilerParams(
             collective_id=0, has_side_effects=True, vmem_limit_bytes=VMEM_BYTES),
     )(predicted_units, product_group[None], product_goal[None], group_outlet_goal, outlet_date_goal)
-    steps = 1
+    steps = 2
     part = items // steps
     same = lambda shape: pl.BlockSpec(shape, lambda i: (0,) * len(shape))
     factor, cat, date, out = pl.pallas_call(

time: 76.9 us -> 76 us (0.988)
  Pallas kernels: 76.1 us -> 75.2 us
where the time goes in v7:
time: 76 us; the launch traced here: 75.9 us
  Pallas kernels  75.2 us (99%)
    pallas_call x1, Pallas kernels, shards(): pl.pallas_call(functools.partial(kernel, n_item, n_store, sent_cats), out...  72.9 us
    pallas_call x1, Pallas kernels, shards(): pl.pallas_call(finish, grid=(steps,), out_shape=(jax.ShapeDtypeStruct((1,...  2.28 us

profile of v7, /device:TPU:0, one launch (start us, length us, event | category | flops | bytes accessed | tf_op | source)
XLA Modules:
  0.0 75.9 jit_solution(11376788179744448450)
XLA Ops:
  0.6 72.9 %shard_map.84 = (f32[1,128]{1,0:T(1,128)}, f32[64,512]{1,0:T(8,128)}, f32[8,512]{1,0:T(8,128)}, f32[128,512]{1,0:T(8,128)}) custom-call(bf16[128,8,512]{2,1,0:T(8,128)(2,1)} %x_ref.1, s32[1,128]{1,0:T(1,128)} %bitcast.3, f32[1,128]{1,0:T(1,128)} %bitcast.4, f32[64,512]{1,0:T(8,128)} %cat_goal_hbm.1, f32[8,512]{1,0:T(8,128)} %date_goal_hbm.1), custom_call_target="tpu_custom_call" | custom-call | tf_op jit(solution)/shard_map/pallas_call | solution.py:348
  73.6 2.3 %shard_map.85 = (f32[1,128]{1,0:T(1,128)}, f32[64,512]{1,0:T(8,128)}, f32[8,512]{1,0:T(8,128)}, bf16[128,8,512]{2,1,0:T(8,128)(2,1)}) custom-call(bf16[128,8,512]{2,1,0:T(8,128)(2,1)} %x_ref.1, f32[128,512]{1,0:T(8,128)} %get-tuple-element.12.scale_ref, f32[1,128]{1,0:T(1,128)} %get-tuple-element.13.factor_in, f32[64,512]{1,0:T(8,128)} %get-tuple-element.14.cat_in, ...), custom_call_target="tpu_custom_call" | custom-call | tf_op jit(solution)/shard_map/pallas_call | solution.py:393
